TPU v7x, 32 devices: a whole 2x2x4 slice. The times are simulated.
32 devices in a mesh: groups: 2 (over y), dp: 8 (over z, x), tp: 2 (over core).
Axes of the slice: x: 2, y: 2, z: 4, core: 2. Of those that a mesh axis runs over, the one named last changes fastest.
Arguments:
- cache: bfloat16 [32, 1536, 576], P(('groups', 'dp', 'tp')), parts along dimension 0, may hold values from -4 to 4
- lengths: int32 [32], P('groups'), parts along dimension 0, may hold values from 2 to 1535, as said below
- swap_flags: int32 [1, 32], P(None, 'groups'), parts along dimension 1, may hold values from 0 to 1, as said below
- queries: bfloat16 [1, 32, 128, 576], P(None, ('groups', 'dp', 'tp')), parts along dimension 1, may hold values from -20 to 20
- latents: bfloat16 [1, 32, 576], P(None, ('groups', 'dp', 'tp')), parts along dimension 1, may hold values from -4 to 4
- residual: bfloat16 [1, 32, 7168], P(None, ('groups', 'dp', 'tp')), parts along dimension 1, may hold values from -3 to 3
- norm_gain: bfloat16 [7168], replicated, may hold values from 0.5 to 1.5
- value_expand_weight: bfloat16 [128, 512, 128], P(('dp', 'tp')), may hold values from -0.5 to 0.5
- out_proj: bfloat16 [16384, 7168], P(('dp', 'tp')), may hold values from -0.046875 to 0.046875
- gate_weight: bfloat16 [7168, 18432], P(None, ('dp', 'tp')), may hold values from -0.0625 to 0.0625
- up_weight: bfloat16 [7168, 18432], P(None, ('dp', 'tp')), may hold values from -0.0625 to 0.0625
- down_weight: bfloat16 [18432, 7168], P(('dp', 'tp')), may hold values from -0.046875 to 0.046875
Outputs:
- layer_out: bfloat16 [1, 32, 7168], P(None, ('groups', 'dp', 'tp')), parts along dimension 1
- held: bfloat16 [32, 1536, 576], P(('groups', 'dp', 'tp')), parts along dimension 0
There are 2 independent parts, one for each index of `groups`. A program takes and returns all parts, laid end to end along the dimension named above; an argument that names none is the same for every part. Nothing has to cross between parts.
Inputs may be any that keep to these rules, and one draw needn't show every extreme that they name: `lengths`: each row has at least two cached positions, and some row has exactly 1535. `swap_flags`: for each step the flags agree on a slot and its partner slot of that step.
All inputs are finite; a program needn't handle non-finite values.
Results may differ from a plain program's by a relative error of at most 0.0075.
Values may be sent and summed in bfloat16 or wider, within the bound.
No kernel may reach another device: no remote copies, remote signals or barrier semaphores. Data moves between devices by JAX's collectives and lax.ppermute only.
A program may use at most 192 MiB of HBM per device.

v0:
```python
import jax
import jax.numpy as jnp
from jax import lax
from jax.sharding import PartitionSpec as P

LATENT_WIDTH = 512


score_scale = 0.07216878364870322


def from_partner(block, axis, stride):
    count = lax.axis_size(axis)
    route = []
    for low in range(count):
        high = low | 1 << stride
        if high != low and high < count:
            route += [(low, high), (high, low)]
    return lax.ppermute(block, axis, route)


def attend(query_rows, key_rows, live):
    scores = (
        jnp.einsum("rhl,rtl->rht", query_rows, key_rows, preferred_element_type=jnp.float32)
        * score_scale
    )
    positions = jnp.arange(key_rows.shape[1])
    mask = positions[None, None, :] < live[:, None, None]
    scores = jnp.where(mask, scores, -1e30)
    top = jnp.max(scores, axis=-1, keepdims=True)
    weights = jnp.where(mask, jnp.exp(scores - top), 0.0)
    attention_probabilities = (weights / jnp.sum(weights, axis=-1, keepdims=True)).astype(
        jnp.bfloat16
    )
    return jnp.einsum(
        "efw,ewa->efa",
        attention_probabilities,
        key_rows[:, :, :LATENT_WIDTH],
        preferred_element_type=jnp.float32,
    ).astype(jnp.bfloat16)


def append_entry(key_rows, entry, where_pos):
    positions = jnp.arange(key_rows.shape[1], dtype=jnp.int32)
    write = positions[None, :] == where_pos[:, None]
    return jnp.where(write[:, :, None], entry[:, None, :], key_rows)


def local(
    cache,
    lengths,
    swap_flags,
    queries,
    latents,
    residual,
    norm_gain,
    value_expand_weight,
    out_proj,
    gate_weight,
    up_weight,
    down_weight,
):
    ranks = lax.axis_size(("dp", "tp"))
    top_bit = ranks.bit_length() - 1
    rows_dev = cache.shape[0]
    rows_all = rows_dev * ranks
    first = lax.axis_index(("dp", "tp")) * rows_dev
    slots = jnp.arange(rows_all, dtype=jnp.int32)
    rowat = slots
    step = 0
    bit = top_bit - 1 - step
    partner = (slots // rows_dev ^ 1 << bit) * rows_dev + slots % rows_dev
    moved = jnp.where(swap_flags[step] == 1, partner, slots)
    rowat = rowat[moved]
    rowat_list = [rowat]
    flag_local = [lax.dynamic_slice_in_dim(swap_flags[step], first, rows_dev, 0)]
    gain = norm_gain.astype(jnp.float32)
    current = cache
    step = 0
    other = from_partner(current, ("dp", "tp"), top_bit - 1 - step)
    current = jnp.where(flag_local[step][:, None, None] == 1, other, current)
    local_len = lax.dynamic_slice_in_dim(lengths[rowat_list[step]], first, rows_dev, 0)
    query_now = queries[step]
    entry = latents[step]
    current = append_entry(current, entry, local_len + step)
    context_rows = attend(query_now, current, local_len + step + 1)
    per_head_rows = lax.all_to_all(
        context_rows, ("dp", "tp"), split_axis=1, concat_axis=0, tiled=True
    )
    value_rows = jnp.einsum(
        "wzl,zlb->wzb", per_head_rows, value_expand_weight, preferred_element_type=jnp.float32
    ).astype(jnp.bfloat16)
    flat = value_rows.reshape(rows_all, value_rows.shape[1] * value_rows.shape[2])
    attn_out = lax.psum_scatter(
        jnp.dot(flat, out_proj, preferred_element_type=jnp.float32),
        ("dp", "tp"),
        scatter_dimension=0,
        tiled=True,
    )
    state = residual[step].astype(jnp.float32) + attn_out
    normed = (
        state * lax.rsqrt(jnp.mean(state * state, axis=-1, keepdims=True) + 1e-06) * gain
    ).astype(jnp.bfloat16)
    piece = lax.all_gather(normed, ("dp", "tp"), axis=0, tiled=True)
    gate = jnp.dot(piece, gate_weight, preferred_element_type=jnp.float32)
    upper = jnp.dot(piece, up_weight, preferred_element_type=jnp.float32)
    hidden = (jax.nn.silu(gate) * upper).astype(jnp.bfloat16)
    partial_value = jnp.dot(hidden, down_weight, preferred_element_type=jnp.float32)
    ffn_out = lax.psum_scatter(partial_value, ("dp", "tp"), scatter_dimension=0, tiled=True)
    results = [(state + ffn_out).astype(jnp.bfloat16)]
    return (jnp.stack(results), current)


def solution(mesh):
    placed = (
        P(("groups", "dp", "tp"), None, None),
        P("groups"),
        P(None, "groups"),
        P(None, ("groups", "dp", "tp"), None, None),
        P(None, ("groups", "dp", "tp"), None),
        P(None, ("groups", "dp", "tp"), None),
        P(),
        P(("dp", "tp"), None, None),
        P(("dp", "tp"), None),
        P(None, ("dp", "tp")),
        P(None, ("dp", "tp")),
        P(("dp", "tp"), None),
    )
    return jax.shard_map(
        local,
        mesh=mesh,
        in_specs=placed,
        out_specs=(P(None, ("groups", "dp", "tp"), None), P(("groups", "dp", "tp"), None, None)),
        check_vma=False,
    )
```

profile of v0, /device:TPU:0, one launch (start us, length us, event | category | flops | bytes accessed | tf_op | source)
XLA Modules:
  0.0 351.7 jit_solution(1666131032086214023)
XLA Ops:
  7.2 0.0 copy-start
  7.2 0.0 all-reduce.5.cloned.1.call-start
  7.2 4.1 %collective-permute-start = (bf16[1,1536,576]{1,2,0:T(8,128)(2,1)}, bf16[1,1536,576]{1,2,0:T(8,128)(2,1)S(1)}, u32[]{:S(2)}, u32[]{:S(2)}) collective-permute-start(bf16[1,1536,576]{1,2,0:T(8,128)(2,1)} %param.12), channel_id=1, source_target_pairs={{0,8},{8,0},{1,9},{9,1},{2,10},{10,2},{3,11},{11,3},{4,12},{12,4},... | collective-permute-start | bytes 5308424 | tf_op jit(solution)/shard_map/ppermute | solution.py:19
  11.3 1.2 fusion.37
  12.6 0.7 fusion.34
  13.2 0.7 gather_fusion
  13.9 1.3 gather_fusion.1
  15.2 0.6 dynamic_slice.6
  15.8 0.7 reduce.7
  17.2 0.7 iota_compare_fusion
  17.9 70.2 %collective-permute-done = bf16[1,1536,576]{1,2,0:T(8,128)(2,1)S(1)} collective-permute-done((bf16[1,1536,576]{1,2,0:T(8,128)(2,1)}, bf16[1,1536,576]{1,2,0:T(8,128)(2,1)S(1)}, u32[]{:S(2)}, u32[]{:S(2)}) %collective-permute-start) | collective-permute-done | bytes 1769504 | tf_op jit(solution)/shard_map/ppermute | solution.py:19
  88.1 0.0 copy-start.3
  88.1 1.2 copy-done.3
  89.3 2.4 select_select_fusion
  91.6 0.0 copy-start.2
  91.7 1.9 fusion.38
  93.6 0.0 copy-start.5
  93.6 0.0 copy-start.6
  93.6 0.0 copy-start.4
  93.6 0.3 fusion.7
  93.9 1.0 fusion.5
  94.9 0.2 copy.43
  95.1 0.5 broadcast.168
  95.7 1.4 reduce.8
  97.1 0.1 reshape.170
  97.1 13.6 %all_to_all.12 = bf16[16,2,2048]{2,1,0:T(2,128)(2,1)S(1)} all-to-all(bf16[16,2,2048]{2,1,0:T(2,128)(2,1)S(1)} %reshape.170), channel_id=1, replica_groups=mesh['groups'=2,'dp'=8,'tp'=2] {'dp','tp'}, dimensions={0} | all-to-all | bytes 262144 | tf_op jit(solution)/shard_map/all_to_all | solution.py:87
  110.7 0.1 reshape.171
  110.9 0.0 copy-done
  110.9 0.3 fusion.6
  111.1 8.0 %fusion.28 = f32[16,7168]{1,0:T(8,128)} fusion(bf16[1024,7168]{1,0:T(8,128)(2,1)} %param.20, bf16[8,2,8,128]{3,2,1,0:T(8,128)(2,1)S(1)} %fusion.6), kind=kOutput, calls=%fused_computation.36 | convolution fusion | flops 234881024 | bytes 15171584 | tf_op jit(solution)/shard_map/dot_general | solution.py:95
  119.1 0.0 copy-done.2
  119.1 0.0 all-reduce.5.cloned.1.call-update
  119.2 0.0 all-reduce.7.cloned.1.call-start
  119.2 0.0 copy-done.5
  119.2 0.0 copy-done.6
  119.3 0.6 dynamic-slice.1
  119.9 86.9 %all-reduce.5.cloned.1.call-done = f32[16,7168]{1,0:T(8,128)} async-done(((f32[16,7168]{1,0:T(8,128)}), f32[16,7168]{1,0:T(8,128)}) %all-reduce.5.cloned.1.call-update) | async-done | bytes 458768
  206.8 0.0 copy-done.4
  206.8 2.2 multiply_reduce_fusion
  209.7 22.1 %all-gather = bf16[16,1,7168]{2,1,0:T(2,128)(2,1)S(1)} all-gather(bf16[1,1,7168]{2,1,0:T(2,128)(2,1)S(1)} %convert_bitcast_fusion), channel_id=1, replica_groups=mesh['groups'=2,'dp'=8,'tp'=2] {'dp','tp'}, dimensions={0}, use_global_device_ids=true | all-gather | bytes 243712 | tf_op jit(solution)/shard_map/all_gather | solution.py:104
  231.8 0.0 copy-start.1
  231.8 8.0 %fusion.15 = f32[16,1152]{1,0:T(8,128)S(1)} fusion(bf16[7168,1152]{1,0:T(8,128)(2,1)} %param.21, bf16[16,1,7168]{2,1,0:T(2,128)(2,1)S(1)} %all-gather), kind=kOutput, calls=%fused_computation.23 | convolution fusion | flops 264241152 | bytes 16818176 | tf_op jit(solution)/shard_map/dot_general | solution.py:105
  239.8 15.6 %fusion.8 = f32[16,7168]{1,0:T(8,128)} fusion(bf16[1152,7168]{1,0:T(8,128)(2,1)} %param.23, bf16[7168,1152]{1,0:T(8,128)(2,1)} %param.22, bf16[16,1,7168]{2,1,0:T(2,128)(2,1)S(1)} %all-gather, f32[16,1152]{1,0:T(8,128)S(1)} %fusion.15), kind=kOutput, calls=%fused_computation.17 | convolution fusion | flops 528592896 | bytes 33792000 | tf_op jit(solution)/shard_map/dot_general | solution.py:108
  255.4 0.0 all-reduce.7.cloned.1.call-update
  255.5 87.2 %all-reduce.7.cloned.1.call-done = f32[16,7168]{1,0:T(8,128)} async-done(((f32[16,7168]{1,0:T(8,128)}), f32[16,7168]{1,0:T(8,128)}) %all-reduce.7.cloned.1.call-update) | async-done | bytes 458768
  342.7 2.2 fusion.32
  344.8 0.0 copy-done.1
  (8 shorter events, 0.1 us)
Async XLA Ops:
  7.2 103.7 %copy-start = (bf16[8,512,128]{2,1,0:T(8,128)(2,1)S(1)}, bf16[8,512,128]{2,1,0:T(8,128)(2,1)}, u32[]{:S(2)}) copy-start(bf16[8,512,128]{2,1,0:T(8,128)(2,1)} %param.19) | copy-start | bytes 3145732
  7.2 199.6 %all-reduce.5.cloned.1.call-start = ((), (), s32[]{:S(2)}) async-start(), calls=%async_computation.1 | async-start | bytes 917504
  7.2 80.8 %collective-permute-start = (bf16[1,1536,576]{1,2,0:T(8,128)(2,1)}, bf16[1,1536,576]{1,2,0:T(8,128)(2,1)S(1)}, u32[]{:S(2)}, u32[]{:S(2)}) collective-permute-start(bf16[1,1536,576]{1,2,0:T(8,128)(2,1)} %param.12), channel_id=1, source_target_pairs={{0,8},{8,0},{1,9},{9,1},{2,10},{10,2},{3,11},{11,3},{4,12},{12,4},... | collective-permute-start | bytes 5308424 | tf_op jit(solution)/shard_map/ppermute | solution.py:19
  88.1 1.2 copy-start.3
  91.6 27.5 %copy-start.2 = (bf16[1,1536,576]{1,2,0:T(8,128)(2,1)}, bf16[1,1536,576]{1,2,0:T(8,128)(2,1)S(1)}, u32[]{:S(2)}) copy-start(bf16[1,1536,576]{1,2,0:T(8,128)(2,1)S(1)} %select_select_fusion) | copy-start | bytes 5308420
  93.6 25.6 %copy-start.5 = (bf16[7168]{0:T(1024)(128)(2,1)S(1)}, bf16[7168]{0:T(1024)(128)(2,1)}, u32[]{:S(2)}) copy-start(bf16[7168]{0:T(1024)(128)(2,1)} %param.18) | copy-start | bytes 43012
  93.6 25.7 %copy-start.6 = (u32[32]{0:T(128)S(1)}, u32[32]{0:T(128)}, u32[]{:S(2)}) copy-start(u32[32]{0:T(128)} %constant.74) | copy-start | bytes 388
  93.6 113.2 %copy-start.4 = (bf16[1,1,7168]{2,1,0:T(2,128)(2,1)S(1)}, bf16[1,1,7168]{2,1,0:T(2,128)(2,1)}, u32[]{:S(2)}) copy-start(bf16[1,1,7168]{2,1,0:T(2,128)(2,1)} %param.17) | copy-start | bytes 43012
  119.2 223.5 %all-reduce.7.cloned.1.call-start = ((), (), s32[]{:S(2)}) async-start(), calls=%async_computation.2 | async-start | bytes 917504
  231.8 113.0 %copy-start.1 = (bf16[8,512,128]{2,1,0:T(8,128)(2,1)S(1)}, bf16[8,512,128]{2,1,0:T(8,128)(2,1)}, u32[]{:S(2)}) copy-start(bf16[8,512,128]{2,1,0:T(8,128)(2,1)} %param.19) | copy-start | bytes 3145732
Sparse Core Ops, SparseCore 0:
  119.3 87.4 all-reduce.4
  255.6 87.0 all-reduce.6
where the time goes:
time: 352 us
  waiting for transfers between devices  244 us (69%)
  blocking collectives  35.7 us (10%)
  matrix products  34.8 us (10%)
  between operations  15.6 us (4%)
  other arithmetic  11.8 us (3%)
  local copies, waits for them, and re-layouts  5.35 us (2%)
  starting transfers between devices  4.18 us (1%)
    unnamed x4, waiting for transfers between devices  174 us
    ppermute x1, waiting for transfers between devices, from_partner(): return lax.ppermute(block, axis, route)  70.2 us
    all_gather x1, blocking collectives, local(): piece = lax.all_gather(normed, ('dp', 'tp'), axis=0, tiled=True)  22.1 us
    dot_general x1, matrix products, local(): jnp.dot(hidden, down_weight, preferred_element_type=jnp.float32)  15.6 us
    all_to_all x1, blocking collectives, local(): lax.all_to_all(context_rows, ('dp', 'tp'), split_axis=1, concat_axis=0, t...  13.6 us
    dot_general x1, matrix products, local(): gate = jnp.dot(piece, gate_weight, preferred_element_type=jnp.float32)  8.02 us
    dot_general x1, matrix products, local(): jnp.dot(flat, out_proj, preferred_element_type=jnp.float32)  7.99 us
  transfers between devices with their start and end apart: 3, of which 3 were waited for; matrix products, arithmetic and copies ran while one was open for 2% of the time, Pallas kernels for 0%

commit v1 on v0

v1 whole, which is shorter than its diff:
```python
import jax
import jax.numpy as jnp
from jax import lax
from jax.sharding import PartitionSpec as P

LATENT_WIDTH = 512
AXES = ("dp", "tp")


score_scale = 0.07216878364870322


def swap_bit(block, bit):
    ranks = lax.axis_size(AXES)
    return lax.ppermute(block, AXES, [(rank, rank ^ 1 << bit) for rank in range(ranks)])


def attend(query_rows, key_rows, live):
    scores = (
        jnp.einsum("rhl,rtl->rht", query_rows, key_rows, preferred_element_type=jnp.float32)
        * score_scale
    )
    positions = jnp.arange(key_rows.shape[1])
    mask = positions[None, None, :] < live[:, None, None]
    scores = jnp.where(mask, scores, -1e30)
    top = jnp.max(scores, axis=-1, keepdims=True)
    weights = jnp.where(mask, jnp.exp(scores - top), 0.0)
    attention_probabilities = (weights / jnp.sum(weights, axis=-1, keepdims=True)).astype(
        jnp.bfloat16
    )
    return jnp.einsum(
        "efw,ewa->efa",
        attention_probabilities,
        key_rows[:, :, :LATENT_WIDTH],
        preferred_element_type=jnp.float32,
    ).astype(jnp.bfloat16)


def append_entry(key_rows, entry, where_pos):
    positions = jnp.arange(key_rows.shape[1], dtype=jnp.int32)
    write = positions[None, :] == where_pos[:, None]
    return jnp.where(write[:, :, None], entry[:, None, :], key_rows)


def split_rows(block, bit_value):
    pairs = block.reshape(block.shape[0] // 2, 2, *block.shape[1:])
    keep = lax.dynamic_index_in_dim(pairs, bit_value, 1, keepdims=False)
    send = lax.dynamic_index_in_dim(pairs, 1 - bit_value, 1, keepdims=False)
    return keep, send


def local(
    cache,
    lengths,
    swap_flags,
    queries,
    latents,
    residual,
    norm_gain,
    value_expand_weight,
    out_proj,
    gate_weight,
    up_weight,
    down_weight,
):
    ranks = lax.axis_size(AXES)
    bits = ranks.bit_length() - 1
    rows_dev = cache.shape[0]
    rows_all = rows_dev * ranks
    rank = lax.axis_index(AXES)
    bit_of = [(rank >> bit) & 1 for bit in range(bits)]
    half = rows_all // 2
    top = bits - 1

    flags = swap_flags[0]
    moved_len = jnp.where(flags == 1, jnp.roll(lengths, half), lengths)
    flag_here = lax.dynamic_slice_in_dim(flags, rank * rows_dev, rows_dev, 0) == 1
    len_slot = lax.dynamic_slice_in_dim(moved_len, rank * rows_dev, rows_dev, 0)
    len_own = lax.dynamic_slice_in_dim(lengths, rank * rows_dev, rows_dev, 0)

    query_other = swap_bit(queries[0], top)
    entry_other = swap_bit(latents[0], top)
    query_other, entry_other, cache = lax.optimization_barrier((query_other, entry_other, cache))
    cache_other = swap_bit(cache, top)
    query = jnp.where(flag_here[:, None, None], query_other, queries[0])
    entry = jnp.where(flag_here[:, None], entry_other, latents[0])
    context = attend(query, append_entry(cache, entry, len_own), len_own + 1)

    heads = context.shape[1] // ranks
    per_head = lax.all_to_all(
        context.reshape(rows_dev, ranks, heads, LATENT_WIDTH).swapaxes(0, 1),
        AXES,
        split_axis=0,
        concat_axis=0,
        tiled=True,
    ).reshape(rows_all, heads, LATENT_WIDTH)
    values = jnp.einsum(
        "whl,hlb->whb", per_head, value_expand_weight, preferred_element_type=jnp.float32
    ).astype(jnp.bfloat16)
    values = values.reshape(rows_all, -1)
    values = jnp.where(flags[:, None] == 1, jnp.roll(values, half, axis=0), values)

    partial = jnp.dot(values, out_proj, preferred_element_type=jnp.float32)
    mine = (jnp.arange(rows_all) // rows_dev == rank)[:, None]
    place = jnp.tile(residual[0].astype(jnp.float32), (ranks, 1))
    partial = partial + jnp.where(mine, place, 0.0)

    width = partial.shape[1]
    state = partial.reshape(ranks, rows_dev * width)
    scattered = 0
    for bit in range(bits):
        if state.shape[0] * rows_dev > 8:
            keep, send = split_rows(state, bit_of[bit])
            scattered += 1
        else:
            keep = send = state
        state = keep + swap_bit(send.astype(jnp.bfloat16), bit).astype(jnp.float32)
    state = state.reshape(-1, width)
    gain = norm_gain.astype(jnp.float32)
    normed = (
        state * lax.rsqrt(jnp.mean(state * state, axis=-1, keepdims=True) + 1e-06) * gain
    ).astype(jnp.bfloat16)
    for bit in reversed(range(scattered)):
        normed = jnp.concatenate([normed, swap_bit(normed, bit)], axis=0)
    gate = jnp.dot(normed, gate_weight, preferred_element_type=jnp.float32)
    upper = jnp.dot(normed, up_weight, preferred_element_type=jnp.float32)
    hidden = (jax.nn.silu(gate) * upper).astype(jnp.bfloat16)
    total = jnp.dot(hidden, down_weight, preferred_element_type=jnp.float32)
    for bit in range(scattered):
        keep, send = jnp.split(total, 2, axis=0)
        total = keep + swap_bit(send.astype(jnp.bfloat16), bit).astype(jnp.float32)
    total = total.reshape(-1, rows_dev * width)
    for bit in range(scattered, bits):
        keep, send = split_rows(total, bit_of[bit])
        total = keep + swap_bit(send.astype(jnp.bfloat16), bit).astype(jnp.float32)
    own = lax.dynamic_slice_in_dim(state, (rank >> scattered) * rows_dev, rows_dev, 0)
    layer_out = (own + total.reshape(rows_dev, width)).astype(jnp.bfloat16)

    held = jnp.where(flag_here[:, None, None], cache_other, cache)
    held = append_entry(held, latents[0], len_slot)
    return layer_out[None], held


def solution(mesh):
    placed = (
        P(("groups", "dp", "tp"), None, None),
        P("groups"),
        P(None, "groups"),
        P(None, ("groups", "dp", "tp"), None, None),
        P(None, ("groups", "dp", "tp"), None),
        P(None, ("groups", "dp", "tp"), None),
        P(),
        P(("dp", "tp"), None, None),
        P(("dp", "tp"), None),
        P(None, ("dp", "tp")),
        P(None, ("dp", "tp")),
        P(("dp", "tp"), None),
    )
    return jax.shard_map(
        local,
        mesh=mesh,
        in_specs=placed,
        out_specs=(P(None, ("groups", "dp", "tp"), None), P(("groups", "dp", "tp"), None, None)),
        check_vma=False,
    )
```

time: 352 us -> 176 us (0.50)
  waiting for transfers between devices: 244 us -> 117 us
  blocking collectives: 35.7 us -> 0 us
  between operations: 15.6 us -> 1.57 us
  starting transfers between devices: 4.18 us -> 9.39 us
    unnamed x4 -> x0, waiting for transfers between devices: 174 us -> none
    ppermute x1 -> x12, waiting for transfers between devices: 70.2 us -> 109 us  [swap_bit(): lax.ppermute(block, AXES, [(rank, rank ^ 1 << bit) for rank in range(rank...]
    all_gather x1 -> x0, blocking collectives: 22.1 us -> none  [local(): piece = lax.all_gather(normed, ('dp', 'tp'), axis=0, tiled=True)]
    all_to_all x1 -> x0, blocking collectives: 13.6 us -> none  [local(): lax.all_to_all(context_rows, ('dp', 'tp'), split_axis=1, concat_axis=0, t...]
    all_to_all x0 -> x1, waiting for transfers between devices: none -> 7.81 us  [local(): lax.all_to_all(context.reshape(rows_dev, ranks, heads, LATENT_WIDTH).swap...]
  transfers between devices with their start and end apart: 3 -> 13, of which waited for: 3 -> 12; matrix products, arithmetic and copies ran while one was open for 2% -> 5% of each run, Pallas kernels for 0% -> 0%
where the time goes in v1:
time: 176 us; the launch traced here: 175 us
  waiting for transfers between devices  117 us (66%)
  matrix products  32.8 us (19%)
  other arithmetic  10.6 us (6%)
  starting transfers between devices  9.39 us (5%)
  local copies, waits for them, and re-layouts  4.13 us (2%)
    ppermute x12, waiting for transfers between devices, swap_bit(): lax.ppermute(block, AXES, [(rank, rank ^ 1 << bit) for rank in range(rank...  109 us
    dot_general x1, matrix products, local(): total = jnp.dot(hidden, down_weight, preferred_element_type=jnp.float32)  14.9 us
    dot_general x1, matrix products, local(): upper = jnp.dot(normed, up_weight, preferred_element_type=jnp.float32)  7.92 us
    all_to_all x1, waiting for transfers between devices, local(): lax.all_to_all(context.reshape(rows_dev, ranks, heads, LATENT_WIDTH).swap...  7.81 us
    dot_general x1, matrix products, local(): partial = jnp.dot(values, out_proj, preferred_element_type=jnp.float32)  7.23 us
    ppermute x12, starting transfers between devices, swap_bit(): lax.ppermute(block, AXES, [(rank, rank ^ 1 << bit) for rank in range(rank...  5.88 us
    select_n x1, other arithmetic, append_entry(): return jnp.where(write[:, :, None], entry[:, None, :], key_rows)  3.68 us
  transfers between devices with their start and end apart: 13, of which 12 were waited for; matrix products, arithmetic and copies ran while one was open for 5% of the time, Pallas kernels for 0%

profile of v1, /device:TPU:0, one launch (start us, length us, event | category | flops | bytes accessed | tf_op | source)
XLA Modules:
  0.0 175.3 jit_solution(4085493118239393367)
XLA Ops:
  0.6 4.1 %collective-permute-start = (bf16[1,128,576]{1,2,0:T(8,128)(2,1)}, bf16[1,128,576]{1,2,0:T(8,128)(2,1)S(1)}, u32[]{:S(2)}, u32[]{:S(2)}) collective-permute-start(bf16[1,128,576]{1,2,0:T(8,128)(2,1)} %bitcast.86), channel_id=1, source_target_pairs={{0,8},{1,9},{2,10},{3,11},{4,12},{5,13},{6,14},{7,15},{8,0},{9,1},... | collective-permute-start | bytes 442376 | tf_op jit(solution)/shard_map/ppermute | solution.py:15
  4.7 0.1 collective-permute-start.1
  4.8 7.2 %collective-permute-done.1 = bf16[1,576]{1,0:T(2,128)(2,1)S(1)} collective-permute-done((bf16[1,576]{1,0:T(2,128)(2,1)}, bf16[1,576]{1,0:T(2,128)(2,1)S(1)}, u32[]{:S(2)}, u32[]{:S(2)}) %collective-permute-start.1) | collective-permute-done | bytes 1184 | tf_op jit(solution)/shard_map/ppermute | solution.py:15
  12.1 1.3 dynamic_slice.36
  13.4 1.2 fusion.39
  14.6 0.8 fusion.38
  15.4 0.7 add_select_fusion
  16.2 0.6 dynamic_slice.45
  16.8 0.7 reduce.5
  18.1 1.3 iota_compare_fusion
  19.4 1.4 fusion.29
  20.7 70.2 %collective-permute-done.11 = bf16[1,1536,576]{1,2,0:T(8,128)(2,1)S(1)} collective-permute-done((bf16[1,1536,576]{1,2,0:T(8,128)(2,1)}, bf16[1,1536,576]{1,2,0:T(8,128)(2,1)S(1)}, u32[]{:S(2)}, u32[]{:S(2)}) %collective-permute-start.11) | collective-permute-done | bytes 1769504 | tf_op jit(solution)/shard_map/ppermute | solution.py:15
  90.9 3.7 %select_select_fusion = (bf16[1,1536,576]{1,2,0:T(8,128)(2,1)}, bf16[1,1536,576]{1,2,0:T(8,128)(2,1)S(1)}) fusion(bf16[1,1536,576]{1,2,0:T(8,128)(2,1)S(1)} %collective-permute-done.11, bf16[1,1536,576]{1,2,0:T(8,128)(2,1)} %param.12, pred[]{:T(512)} %bitcast.2, pred[1536]{0:T(1024)(128)(4,1)S(1)} %get-tuple-element.18, bf16[576]{0:T(1024)(128)(2,1)S(1)} %reduce.5, ...), kind=kLoop, calls=%fused_computation.4 | loop fusion | flops 2654208 | bytes 7083265 | tf_op jit(solution)/shard_map/jit(_where)/select_n | solution.py:42
  94.6 1.2 fusion.40
  95.8 0.3 fusion.5
  96.1 1.3 fusion.4
  97.5 3.5 %all-to-all-start = ((bf16[16,1,8,512]{3,2,1,0:T(8,128)(2,1)}), bf16[16,1,8,512]{3,2,1,0:T(8,128)(2,1)S(1)}, u32[]{:S(2)}, u32[]{:S(2)}) async-start(bf16[16,1,8,512]{3,2,1,0:T(8,128)(2,1)} %fusion.4), calls=%async_computation | async-start | bytes 262144 | tf_op jit(solution)/shard_map/all_to_all | solution.py:90
  101.1 7.8 %all-to-all-done = bf16[16,1,8,512]{3,2,1,0:T(8,128)(2,1)S(1)} async-done(((bf16[16,1,8,512]{3,2,1,0:T(8,128)(2,1)}), bf16[16,1,8,512]{3,2,1,0:T(8,128)(2,1)S(1)}, u32[]{:S(2)}, u32[]{:S(2)}) %all-to-all-start) | async-done | bytes 131104 | tf_op jit(solution)/shard_map/all_to_all | solution.py:90
  108.9 0.3 convolution_convert_fusion
  109.2 7.2 %convolution_add_fusion = f32[16,7168]{1,0:T(8,128)S(1)} fusion(bf16[1024,7168]{1,0:T(8,128)(2,1)} %param.20, f32[7168]{0:T(1024)S(1)} %bitcast.87, pred[16]{0:T(512)(128)(4,1)S(1)} %iota_compare_fusion.3, bf16[8,1024]{1,0:T(8,128)(2,1)S(1)} %get-tuple-element.13, bf16[8,1024]{1,0:T(8,128)(2,1)S(1)} %get-tuple-element.12, ...), kind=kOutput, calls=%fused_computation | convolution fusion | flops 235192320 | bytes 15233056 | tf_op jit(solution)/shard_map/dot_general | solution.py:103
  116.4 0.3 reshape.150
  116.7 0.2 constant_dynamic-slice_fusion.4
  116.9 0.1 collective-permute-start.2
  117.0 0.2 constant_dynamic-slice_fusion.5
  117.2 1.1 collective-permute-done.2
  118.4 0.1 collective-permute-start.3
  118.5 5.2 %collective-permute-done.3 = bf16[8,7168]{1,0:T(8,128)(2,1)S(1)} collective-permute-done((bf16[8,7168]{1,0:T(8,128)(2,1)S(1)}, bf16[8,7168]{1,0:T(8,128)(2,1)S(1)}, u32[]{:S(2)}, u32[]{:S(2)}) %collective-permute-start.3) | collective-permute-done | bytes 114720 | tf_op jit(solution)/shard_map/ppermute | solution.py:15
  123.7 0.1 collective-permute-start.4
  123.8 4.8 %collective-permute-done.4 = bf16[8,7168]{1,0:T(8,128)(2,1)S(1)} collective-permute-done((bf16[8,7168]{1,0:T(8,128)(2,1)S(1)}, bf16[8,7168]{1,0:T(8,128)(2,1)S(1)}, u32[]{:S(2)}, u32[]{:S(2)}) %collective-permute-start.4) | collective-permute-done | bytes 114720 | tf_op jit(solution)/shard_map/ppermute | solution.py:15
  128.6 0.4 collective-permute-start.5
  129.0 6.0 %collective-permute-done.5 = bf16[8,7168]{1,0:T(8,128)(2,1)S(1)} collective-permute-done((bf16[8,7168]{1,0:T(8,128)(2,1)S(1)}, bf16[8,7168]{1,0:T(8,128)(2,1)S(1)}, u32[]{:S(2)}, u32[]{:S(2)}) %collective-permute-start.5) | collective-permute-done | bytes 114720 | tf_op jit(solution)/shard_map/ppermute | solution.py:15
  135.0 0.2 multiply_reduce_fusion
  135.2 0.1 multiply_convert_fusion
  135.4 1.3 collective-permute-done.6
  136.7 7.9 %fusion.11 = f32[16,1152]{1,0:T(8,128)S(1)} fusion(bf16[7168,1152]{1,0:T(8,128)(2,1)} %param.22, bf16[8,7168]{1,0:T(8,128)(2,1)S(1)} %collective-permute-done.6, bf16[8,7168]{1,0:T(8,128)(2,1)S(1)} %multiply_convert_fusion), kind=kOutput, calls=%fused_computation.29 | convolution fusion | flops 264699904 | bytes 16818176 | tf_op jit(solution)/shard_map/dot_general | solution.py:126
  144.7 14.9 %fusion.21 = f32[16,7168]{1,0:T(8,128)S(1)} fusion(bf16[1152,7168]{1,0:T(8,128)(2,1)} %param.23, f32[16,1152]{1,0:T(8,128)S(1)} %fusion.11, bf16[7168,1152]{1,0:T(8,128)(2,1)} %param.21, bf16[8,7168]{1,0:T(8,128)(2,1)S(1)} %collective-permute-done.6, bf16[8,7168]{1,0:T(8,128)(2,1)S(1)} %multiply_convert_fusion), kind=kOutput, calls=%fused_computation.44 | convolution fusion | flops 529051648 | bytes 33792000 | tf_op jit(solution)/shard_map/dot_general | solution.py:128
  159.6 0.2 collective-permute-start.7
  159.8 1.2 collective-permute-done.7
  161.0 0.1 reshape.151
  161.1 0.1 constant_dynamic-slice_fusion.2
  161.3 0.7 collective-permute-start.8
  162.0 0.1 constant_dynamic-slice_fusion.3
  162.1 3.5 %collective-permute-done.8 = bf16[4,7168]{1,0:T(4,128)(2,1)S(1)} collective-permute-done((bf16[4,7168]{1,0:T(4,128)(2,1)S(1)}, bf16[4,7168]{1,0:T(4,128)(2,1)S(1)}, u32[]{:S(2)}, u32[]{:S(2)}) %collective-permute-start.8) | collective-permute-done | bytes 57376 | tf_op jit(solution)/shard_map/ppermute | solution.py:15
  165.6 0.1 reshape.152
  165.9 3.8 %collective-permute-done.9 = bf16[2,7168]{1,0:T(2,128)(2,1)S(1)} collective-permute-done((bf16[2,7168]{1,0:T(2,128)(2,1)S(1)}, bf16[2,7168]{1,0:T(2,128)(2,1)S(1)}, u32[]{:S(2)}, u32[]{:S(2)}) %collective-permute-start.9) | collective-permute-done | bytes 28704 | tf_op jit(solution)/shard_map/ppermute | solution.py:15
  169.8 0.1 collective-permute-start.10
  169.9 4.8 %collective-permute-done.10 = bf16[1,7168]{1,0:T(2,128)(2,1)S(1)} collective-permute-done((bf16[1,7168]{1,0:T(2,128)(2,1)S(1)}, bf16[1,7168]{1,0:T(2,128)(2,1)S(1)}, u32[]{:S(2)}, u32[]{:S(2)}) %collective-permute-start.10) | collective-permute-done | bytes 14368 | tf_op jit(solution)/shard_map/ppermute | solution.py:15
  174.7 0.7 convert_bitcast_fusion
  (36 shorter events, 0.8 us)
Async XLA Ops:
  0.6 108.2 %copy-start = (bf16[8,512,128]{2,1,0:T(8,128)(2,1)S(1)}, bf16[8,512,128]{2,1,0:T(8,128)(2,1)}, u32[]{:S(2)}) copy-start(bf16[8,512,128]{2,1,0:T(8,128)(2,1)} %param.19) | copy-start | bytes 3145732
  0.6 11.4 %collective-permute-start = (bf16[1,128,576]{1,2,0:T(8,128)(2,1)}, bf16[1,128,576]{1,2,0:T(8,128)(2,1)S(1)}, u32[]{:S(2)}, u32[]{:S(2)}) collective-permute-start(bf16[1,128,576]{1,2,0:T(8,128)(2,1)} %bitcast.86), channel_id=1, source_target_pairs={{0,8},{1,9},{2,10},{3,11},{4,12},{5,13},{6,14},{7,15},{8,0},{9,1},... | collective-permute-start | bytes 442376 | tf_op jit(solution)/shard_map/ppermute | solution.py:15
  4.7 7.3 %collective-permute-start.1 = (bf16[1,576]{1,0:T(2,128)(2,1)}, bf16[1,576]{1,0:T(2,128)(2,1)S(1)}, u32[]{:S(2)}, u32[]{:S(2)}) collective-permute-start(bf16[1,576]{1,0:T(2,128)(2,1)} %bitcast.91), channel_id=1, source_target_pairs={{0,8},{1,9},{2,10},{3,11},{4,12},{5,13},{6,14},{7,15},{8,0},{9,1},... | collective-permute-start | bytes 3464 | tf_op jit(solution)/shard_map/ppermute | solution.py:15
  12.1 78.8 %collective-permute-start.11 = (bf16[1,1536,576]{1,2,0:T(8,128)(2,1)}, bf16[1,1536,576]{1,2,0:T(8,128)(2,1)S(1)}, u32[]{:S(2)}, u32[]{:S(2)}) collective-permute-start(bf16[1,1536,576]{1,2,0:T(8,128)(2,1)} %param.12), channel_id=1, source_target_pairs={{0,8},{1,9},{2,10},{3,11},{4,12},{5,13},{6,14},{7,15},{8,0},{9,1},... | collective-permute-start | bytes 5308424 | tf_op jit(solution)/shard_map/ppermute | solution.py:15
  90.9 3.7 %copy-start.2 = (bf16[1,1,128,576]{2,3,1,0:T(8,128)(2,1)S(1)}, bf16[1,1,128,576]{2,3,1,0:T(8,128)(2,1)}, u32[]{:S(2)}) copy-start(bf16[1,1,128,576]{2,3,1,0:T(8,128)(2,1)} %param.15) | copy-start | bytes 442372
  96.1 4.9 %copy-start.3 = (bf16[1,1,7168]{2,1,0:T(2,128)(2,1)S(1)}, bf16[1,1,7168]{2,1,0:T(2,128)(2,1)}, u32[]{:S(2)}) copy-start(bf16[1,1,7168]{2,1,0:T(2,128)(2,1)} %param.17) | copy-start | bytes 43012
  96.1 4.9 %copy-start.5 = (s32[1,16]{1,0:T(1,128)S(1)}, s32[1,16]{1,0:T(1,128)}, u32[]{:S(2)}) copy-start(s32[1,16]{1,0:T(1,128)} %param.14) | copy-start | bytes 196
  97.5 11.4 %all-to-all-start = ((bf16[16,1,8,512]{3,2,1,0:T(8,128)(2,1)}), bf16[16,1,8,512]{3,2,1,0:T(8,128)(2,1)S(1)}, u32[]{:S(2)}, u32[]{:S(2)}) async-start(bf16[16,1,8,512]{3,2,1,0:T(8,128)(2,1)} %fusion.4), calls=%async_computation | async-start | bytes 262144 | tf_op jit(solution)/shard_map/all_to_all | solution.py:90
  116.4 12.6 %copy-start.4 = (bf16[7168]{0:T(1024)(128)(2,1)S(1)}, bf16[7168]{0:T(1024)(128)(2,1)}, u32[]{:S(2)}) copy-start(bf16[7168]{0:T(1024)(128)(2,1)} %param.18) | copy-start | bytes 43012
  116.9 1.4 collective-permute-start.2
  118.4 5.3 %collective-permute-start.3 = (bf16[8,7168]{1,0:T(8,128)(2,1)S(1)}, bf16[8,7168]{1,0:T(8,128)(2,1)S(1)}, u32[]{:S(2)}, u32[]{:S(2)}) collective-permute-start(bf16[8,7168]{1,0:T(8,128)(2,1)S(1)} %fusion.37), channel_id=1, source_target_pairs={{0,2},{1,3},{2,0},{3,1},{4,6},{5,7},{6,4},{7,5},{8,10},{9,11},{10,... | collective-permute-start | bytes 344072 | tf_op jit(solution)/shard_map/ppermute | solution.py:15
  123.7 4.9 %collective-permute-start.4 = (bf16[8,7168]{1,0:T(8,128)(2,1)S(1)}, bf16[8,7168]{1,0:T(8,128)(2,1)S(1)}, u32[]{:S(2)}, u32[]{:S(2)}) collective-permute-start(bf16[8,7168]{1,0:T(8,128)(2,1)S(1)} %fusion.10), channel_id=1, source_target_pairs={{0,4},{1,5},{2,6},{3,7},{4,0},{5,1},{6,2},{7,3},{8,12},{9,13},{10,... | collective-permute-start | bytes 344072 | tf_op jit(solution)/shard_map/ppermute | solution.py:15
  128.6 6.4 %collective-permute-start.5 = (bf16[8,7168]{1,0:T(8,128)(2,1)S(1)}, bf16[8,7168]{1,0:T(8,128)(2,1)S(1)}, u32[]{:S(2)}, u32[]{:S(2)}) collective-permute-start(bf16[8,7168]{1,0:T(8,128)(2,1)S(1)} %fusion.19), channel_id=1, source_target_pairs={{0,8},{1,9},{2,10},{3,11},{4,12},{5,13},{6,14},{7,15},{8,0},{9,1},... | collective-permute-start | bytes 344072 | tf_op jit(solution)/shard_map/ppermute | solution.py:15
  135.4 1.4 collective-permute-start.6
  144.7 30.7 %copy-start.1 = (bf16[8,512,128]{2,1,0:T(8,128)(2,1)S(1)}, bf16[8,512,128]{2,1,0:T(8,128)(2,1)}, u32[]{:S(2)}) copy-start(bf16[8,512,128]{2,1,0:T(8,128)(2,1)} %param.19) | copy-start | bytes 3145732
  159.6 1.4 collective-permute-start.7
  161.3 4.2 %collective-permute-start.8 = (bf16[4,7168]{1,0:T(4,128)(2,1)S(1)}, bf16[4,7168]{1,0:T(4,128)(2,1)S(1)}, u32[]{:S(2)}, u32[]{:S(2)}) collective-permute-start(bf16[4,7168]{1,0:T(4,128)(2,1)S(1)} %bitcast.89), channel_id=1, source_target_pairs={{0,2},{1,3},{2,0},{3,1},{4,6},{5,7},{6,4},{7,5},{8,10},{9,11},{10,... | collective-permute-start | bytes 172040 | tf_op jit(solution)/shard_map/ppermute | solution.py:15
  165.8 3.9 %collective-permute-start.9 = (bf16[2,7168]{1,0:T(2,128)(2,1)S(1)}, bf16[2,7168]{1,0:T(2,128)(2,1)S(1)}, u32[]{:S(2)}, u32[]{:S(2)}) collective-permute-start(bf16[2,7168]{1,0:T(2,128)(2,1)S(1)} %bitcast.90), channel_id=1, source_target_pairs={{0,4},{1,5},{2,6},{3,7},{4,0},{5,1},{6,2},{7,3},{8,12},{9,13},{10,... | collective-permute-start | bytes 86024 | tf_op jit(solution)/shard_map/ppermute | solution.py:15
  169.8 4.8 %collective-permute-start.10 = (bf16[1,7168]{1,0:T(2,128)(2,1)S(1)}, bf16[1,7168]{1,0:T(2,128)(2,1)S(1)}, u32[]{:S(2)}, u32[]{:S(2)}) collective-permute-start(bf16[1,7168]{1,0:T(2,128)(2,1)S(1)} %dynamic-slice_convert_fusion), channel_id=1, source_target_pairs={{0,8},{1,9},{2,10},{3,11},{4,12},{5,13},{6,14},{7,15},{8,0},{9,1},... | collective-permute-start | bytes 43016 | tf_op jit(solution)/shard_map/ppermute | solution.py:15
